TPU v7x, 32 devices: a whole 2x2x4 slice. The times are simulated.
32 devices in a mesh: dp: 2 (over core), row: 4 (over y, x), col: 4 (over z).
Axes of the slice: x: 2, y: 2, z: 4, core: 2. Of those that a mesh axis runs over, the one named last changes fastest.
Arguments:
- states: float32 [5120, 1024], P(('dp', 'row'), 'col'), may hold values from -6 to 6
- teacher: bfloat16 [5120, 1024], P(('dp', 'row'), 'col'), may hold values from -6 to 6
- cotangent: float32 [5120, 1024], P(('dp', 'row'), 'col'), may hold values from -6 to 6
- lengths: int32 [16], P(('dp', 'row')), may hold values from 256 to 320
- norm_gain: float32 [2, 2, 1024], P(None, None, 'col'), may hold values from 0.5 to 1.5
- norm_bias: float32 [2, 2, 1024], P(None, None, 'col'), may hold values from -2 to 2
- in_weight: bfloat16 [2, 1024, 3, 1024], P(None, 'row', None, 'col'), may hold values from -0.1875 to 0.1875
- in_bias: float32 [2, 2, 1024], P(None, None, 'col'), may hold values from -2 to 2
- proj_weight: bfloat16 [2, 1024, 1024], P(None, 'col', 'row'), may hold values from -0.75 to 0.75
- proj_bias: float32 [2, 1024], P(None, 'col'), may hold values from -2 to 2
- up_weight: bfloat16 [2, 1024, 4096], P(None, 'row', 'col'), may hold values from -0.1875 to 0.1875
- up_bias: float32 [2, 4096], P(None, 'col'), may hold values from -2 to 2
- down_weight: bfloat16 [2, 4096, 1024], P(None, 'col', 'row'), may hold values from -0.125 to 0.125
- down_bias: float32 [2, 1024], P(None, 'col'), may hold values from -2 to 2
Outputs:
- loss_value: float32 [], replicated
- output: float32 [5120, 1024], P(('dp', 'row'), 'col')
- input_grad: float32 [5120, 1024], P(('dp', 'row'), 'col')
- norm_gain_grad: float32 [2, 2, 1024], P(None, None, 'col')
- norm_bias_grad: float32 [2, 2, 1024], P(None, None, 'col')
- in_weight_grad: float32 [2, 1024, 3, 1024], P(None, 'row', None, 'col')
- in_bias_grad: float32 [2, 2, 1024], P(None, None, 'col')
- proj_weight_grad: float32 [2, 1024, 1024], P(None, 'col', 'row')
- proj_bias_grad: float32 [2, 1024], P(None, 'col')
- up_weight_grad: float32 [2, 1024, 4096], P(None, 'row', 'col')
- up_bias_grad: float32 [2, 4096], P(None, 'col')
- down_weight_grad: float32 [2, 4096, 1024], P(None, 'col', 'row')
- down_bias_grad: float32 [2, 1024], P(None, 'col')
Inputs may be any that keep to these rules, and one draw needn't show every extreme that they name: `lengths`: number of valid slots of a sequence; slots from that number on are padding.
All inputs are finite; a program needn't handle non-finite values.
Results may differ from a plain program's by a relative error of at most 0.013.
Values may be sent and summed in bfloat16 or wider, within the bound.
No kernel may reach another device: no remote copies, remote signals or barrier semaphores. Data moves between devices by JAX's collectives and lax.ppermute only.
A program may use at most 192 MiB of HBM per device.

v0:
```python
import jax
import jax.numpy as jnp
from jax import lax
from jax.sharding import PartitionSpec as P

HEAD_DIM = 64
LAYERS = 2
epsilon = 1e-06
fill_value = -1e30


def gelu_exact(inputs):
    return jax.nn.gelu(inputs, approximate=False)


def feature_rows(partial_value):
    return lax.psum_scatter(partial_value, "col", scatter_dimension=1, tiled=True)


def gradient_rows(partial_value):
    return lax.psum_scatter(
        partial_value.astype(jnp.bfloat16), "col", scatter_dimension=1, tiled=True
    ).astype(jnp.float32)


def gather_gradient(gradient):
    return lax.all_gather(gradient, "col", axis=1, tiled=True)


def norm_shares(inputs, gains, shifts, model_width):
    totals = lax.psum((jnp.sum(inputs, axis=1), jnp.sum(inputs * inputs, axis=1)), "col")
    centre = (totals[0] / model_width)[:, None]
    rscale = lax.rsqrt((totals[1] / model_width)[:, None] - centre * centre + epsilon)
    standard = (inputs - centre) * rscale
    normed = lax.all_gather(
        (standard * gains + shifts).astype(jnp.bfloat16), "col", axis=1, tiled=True
    )
    return (normed, standard, rscale)


def norm_backward(grad_share, standard, rscale, gains, model_width):
    scaled = grad_share * gains
    sums = lax.psum((jnp.sum(scaled, axis=1), jnp.sum(scaled * standard, axis=1)), "col")
    grad_input = rscale * (
        scaled - sums[0][:, None] / model_width - standard * sums[1][:, None] / model_width
    )
    return (grad_input, jnp.sum(grad_share * standard, axis=0), jnp.sum(grad_share, axis=0))


def split_heads(flat_rows, seq_here):
    return flat_rows.reshape(
        seq_here, flat_rows.shape[0] // seq_here, flat_rows.shape[1] // HEAD_DIM, HEAD_DIM
    )


def attention_scores(queries, key_block, validity, score_scale):
    scores = (
        jnp.einsum("sqhe,skhe->shqk", queries, key_block, preferred_element_type=jnp.float32)
        * score_scale
    )
    return jnp.where(validity[:, None, None, :], scores, fill_value)


def attend(queries, key_block, values, validity, score_scale):
    scores = attention_scores(queries, key_block, validity, score_scale)
    maximum = jnp.max(scores, axis=-1, keepdims=True)
    exponent = jnp.exp(scores - maximum)
    total_mass = jnp.sum(exponent, axis=-1, keepdims=True)
    attention = (exponent / total_mass).astype(jnp.bfloat16)
    mixture = jnp.einsum("shqk,skhe->sqhe", attention, values, preferred_element_type=jnp.float32)
    return (mixture, maximum + jnp.log(total_mass))


def attend_back(queries, key_block, values, validity, score_scale, logsum, grad_mixture):
    scores = attention_scores(queries, key_block, validity, score_scale)
    chance = jnp.exp(scores - logsum)
    grad_values = jnp.einsum(
        "shqk,sqhe->skhe",
        chance.astype(jnp.bfloat16),
        grad_mixture,
        preferred_element_type=jnp.float32,
    )
    grad_chance = jnp.einsum(
        "sqhe,skhe->shqk", grad_mixture, values, preferred_element_type=jnp.float32
    )
    grad_scores = (
        chance * (grad_chance - jnp.sum(grad_chance * chance, axis=-1, keepdims=True))
    ).astype(jnp.bfloat16)
    grad_queries = (
        jnp.einsum("shqk,skhe->sqhe", grad_scores, key_block, preferred_element_type=jnp.float32)
        * score_scale
    )
    grad_keys = (
        jnp.einsum("shqk,sqhe->skhe", grad_scores, queries, preferred_element_type=jnp.float32)
        * score_scale
    )
    return (grad_queries, grad_keys, grad_values)


def body(
    states,
    teacher,
    cotangent,
    lengths,
    norm_gain,
    norm_bias,
    in_weight,
    in_bias,
    proj_weight,
    proj_bias,
    up_weight,
    up_bias,
    down_weight,
    down_bias,
):
    token_rows = states.shape[0]
    share_width = states.shape[1]
    model_width = share_width * lax.axis_size("col")
    seq_here = lengths.shape[0]
    slot_count = token_rows // seq_here
    score_scale = HEAD_DIM ** (-0.5)
    positions = jnp.arange(slot_count, dtype=jnp.int32)
    validity = positions[None, :] < lengths[:, None]
    row_mask = validity.reshape(token_rows, 1).astype(jnp.float32)
    current = states
    records = []
    for layer_index in range(LAYERS):
        fetched = (
            lax.all_gather(in_weight[layer_index], "row", axis=0, tiled=True),
            lax.all_gather(proj_weight[layer_index], "row", axis=1, tiled=True),
            lax.all_gather(up_weight[layer_index], "row", axis=0, tiled=True),
            lax.all_gather(down_weight[layer_index], "row", axis=1, tiled=True),
        )
        in_full, proj_full, up_full, down_full = fetched
        normed_one, standard_one, rscale_one = norm_shares(
            current, norm_gain[layer_index, 0], norm_bias[layer_index, 0], model_width
        )
        projected = jnp.einsum(
            "td,dpe->tpe", normed_one, in_full, preferred_element_type=jnp.float32
        )
        queries = split_heads(
            (projected[:, 0] + in_bias[layer_index, 0]).astype(jnp.bfloat16), seq_here
        )
        key_block = split_heads(projected[:, 1].astype(jnp.bfloat16), seq_here)
        values = split_heads(
            (projected[:, 2] + in_bias[layer_index, 1]).astype(jnp.bfloat16), seq_here
        )
        mixture, logsum = attend(queries, key_block, values, validity, score_scale)
        attended = mixture.reshape(token_rows, share_width).astype(jnp.bfloat16)
        attn_partial = jnp.dot(attended, proj_full, preferred_element_type=jnp.float32)
        middle = current + feature_rows(attn_partial) + proj_bias[layer_index]
        normed_two, standard_two, rscale_two = norm_shares(
            middle, norm_gain[layer_index, 1], norm_bias[layer_index, 1], model_width
        )
        hidden_pre = (
            jnp.dot(normed_two, up_full, preferred_element_type=jnp.float32) + up_bias[layer_index]
        )
        hidden = gelu_exact(hidden_pre).astype(jnp.bfloat16)
        down_partial = jnp.dot(hidden, down_full, preferred_element_type=jnp.float32)
        records.append(
            (
                fetched,
                normed_one,
                standard_one,
                rscale_one,
                queries,
                key_block,
                values,
                logsum,
                attended,
                normed_two,
                standard_two,
                rscale_two,
                hidden_pre,
                hidden,
            )
        )
        branch = feature_rows(down_partial) + down_bias[layer_index]
        current = (middle + branch) * row_mask
    residue = current - teacher.astype(jnp.float32)
    local_squared = jnp.sum(residue * residue * row_mask)
    local_count = jnp.where(lax.axis_index("col") == 0, jnp.sum(row_mask), 0.0)
    token_total, squared_total = lax.psum((local_count, local_squared), ("dp", "row", "col"))
    loss_value = squared_total / (token_total * model_width)
    factor = token_rows * lax.axis_size("dp") * lax.axis_size("row") / token_total
    grad_current = cotangent + 2.0 * factor * residue * row_mask
    results = [None] * LAYERS
    for layer_index in reversed(range(LAYERS)):
        (
            fetched,
            normed_one,
            standard_one,
            rscale_one,
            queries,
            key_block,
            values,
            logsum,
            attended,
            normed_two,
            standard_two,
            rscale_two,
            hidden_pre,
            hidden,
        ) = records[layer_index]
        in_full, proj_full, up_full, down_full = fetched
        grad_two = grad_current * row_mask
        grad_two_low = grad_two.astype(jnp.bfloat16)
        down_bias_part = jnp.sum(grad_two_low.astype(jnp.float32), axis=0)
        grad_two_rows = gather_gradient(grad_two_low)
        down_part = jnp.einsum(
            "tf,td->fd", hidden, grad_two_rows, preferred_element_type=jnp.float32
        )
        grad_hidden = jnp.einsum(
            "td,fd->tf", grad_two_rows, down_full, preferred_element_type=jnp.float32
        )
        ignored, gelu_pull = jax.vjp(gelu_exact, hidden_pre)
        grad_pre_low = gelu_pull(grad_hidden)[0].astype(jnp.bfloat16)
        up_bias_part = jnp.sum(grad_pre_low.astype(jnp.float32), axis=0)
        up_part = jnp.einsum(
            "td,tf->df", normed_two, grad_pre_low, preferred_element_type=jnp.float32
        )
        grad_normed_two = gradient_rows(
            jnp.einsum("tf,df->td", grad_pre_low, up_full, preferred_element_type=jnp.float32)
        )
        grad_norm_two, gain_part_two, shift_part_two = norm_backward(
            grad_normed_two, standard_two, rscale_two, norm_gain[layer_index, 1], model_width
        )
        grad_middle = grad_two + grad_norm_two
        grad_one_low = grad_middle.astype(jnp.bfloat16)
        proj_bias_part = jnp.sum(grad_one_low.astype(jnp.float32), axis=0)
        grad_one_rows = gather_gradient(grad_one_low)
        proj_part = jnp.einsum(
            "te,td->ed", attended, grad_one_rows, preferred_element_type=jnp.float32
        )
        grad_attended = jnp.einsum(
            "td,ed->te", grad_one_rows, proj_full, preferred_element_type=jnp.float32
        ).astype(jnp.bfloat16)
        grad_queries, grad_keys, grad_values = attend_back(
            queries,
            key_block,
            values,
            validity,
            score_scale,
            logsum,
            split_heads(grad_attended, seq_here),
        )
        grad_triple = jnp.stack(
            [
                grad_queries.reshape(token_rows, share_width),
                grad_keys.reshape(token_rows, share_width),
                grad_values.reshape(token_rows, share_width),
            ],
            axis=1,
        ).astype(jnp.bfloat16)
        in_part = jnp.einsum(
            "td,tpe->dpe", normed_one, grad_triple, preferred_element_type=jnp.float32
        )
        in_bias_part = jnp.stack(
            [
                jnp.sum(grad_triple[:, 0].astype(jnp.float32), axis=0),
                jnp.sum(grad_triple[:, 2].astype(jnp.float32), axis=0),
            ]
        )
        grad_normed_one = gradient_rows(
            jnp.einsum("tpe,dpe->td", grad_triple, in_full, preferred_element_type=jnp.float32)
        )
        grad_norm_one, gain_part_one, shift_part_one = norm_backward(
            grad_normed_one, standard_one, rscale_one, norm_gain[layer_index, 0], model_width
        )
        grad_current = grad_middle + grad_norm_one
        blocks = (
            lax.psum_scatter(
                in_part.astype(jnp.bfloat16), "row", scatter_dimension=0, tiled=True
            ).astype(jnp.float32),
            lax.psum_scatter(
                proj_part.astype(jnp.bfloat16), "row", scatter_dimension=1, tiled=True
            ).astype(jnp.float32),
            lax.psum_scatter(
                up_part.astype(jnp.bfloat16), "row", scatter_dimension=0, tiled=True
            ).astype(jnp.float32),
            lax.psum_scatter(
                down_part.astype(jnp.bfloat16), "row", scatter_dimension=1, tiled=True
            ).astype(jnp.float32),
        )
        blocks = (
            lax.psum(blocks[0].astype(jnp.bfloat16), "dp").astype(jnp.float32),
            lax.psum(blocks[1].astype(jnp.bfloat16), "dp").astype(jnp.float32),
            lax.psum(blocks[2].astype(jnp.bfloat16), "dp").astype(jnp.float32),
            lax.psum(blocks[3].astype(jnp.bfloat16), "dp").astype(jnp.float32),
        )
        vectors = lax.psum(
            (
                jnp.stack([gain_part_one, gain_part_two]),
                jnp.stack([shift_part_one, shift_part_two]),
                in_bias_part,
                proj_bias_part,
                up_bias_part,
                down_bias_part,
            ),
            ("dp", "row"),
        )
        results[layer_index] = (
            vectors[0],
            vectors[1],
            blocks[0],
            vectors[2],
            blocks[1],
            vectors[3],
            blocks[2],
            vectors[4],
            blocks[3],
            vectors[5],
        )
    stacked = [
        jnp.stack([results[layer_index][member] for layer_index in range(LAYERS)])
        for member in range(10)
    ]
    return (
        loss_value,
        current,
        grad_current,
        stacked[0],
        stacked[1],
        stacked[2],
        stacked[3],
        stacked[4],
        stacked[5],
        stacked[6],
        stacked[7],
        stacked[8],
        stacked[9],
    )


def solution(mesh):
    in_specs = (
        P(("dp", "row"), "col"),
        P(("dp", "row"), "col"),
        P(("dp", "row"), "col"),
        P(("dp", "row")),
        P(None, None, "col"),
        P(None, None, "col"),
        P(None, "row", None, "col"),
        P(None, None, "col"),
        P(None, "col", "row"),
        P(None, "col"),
        P(None, "row", "col"),
        P(None, "col"),
        P(None, "col", "row"),
        P(None, "col"),
    )
    out_specs = (
        P(),
        P(("dp", "row"), "col"),
        P(("dp", "row"), "col"),
        P(None, None, "col"),
        P(None, None, "col"),
        P(None, "row", None, "col"),
        P(None, None, "col"),
        P(None, "col", "row"),
        P(None, "col"),
        P(None, "row", "col"),
        P(None, "col"),
        P(None, "col", "row"),
        P(None, "col"),
    )
    return jax.shard_map(body, mesh=mesh, in_specs=in_specs, out_specs=out_specs, check_vma=False)
```

profile of v0, /device:TPU:0, one launch (start us, length us, event | category | flops | bytes accessed | tf_op | source)
XLA Modules:
  0.0 1360.7 jit_solution(17156937366289661022)
XLA Ops:
  11.2 13.7 %all-reduce.9 = (f32[640]{0:T(1024)S(1)}, f32[640]{0:T(1024)S(1)}) all-reduce(f32[640]{0:T(1024)S(1)} %get-tuple-element.28, f32[640]{0:T(1024)S(1)} %get-tuple-element.27), channel_id=1, replica_groups=mesh['dp'=2,'row'=4,'col'=4] {'col'}, use_global_device_ids=true, to_apply=%region_3.0 | all-reduce | flops 1280 | bytes 10240 | tf_op jit(solution)/shard_map/psum | solution.py:31
  30.7 12.9 all-gather.1
  44.3 14.6 %all-gather.23.cloned.1.call-done = bf16[640,1024]{1,0:T(8,128)(2,1)} async-done(((bf16[640,256]{1,0:T(8,128)(2,1)}), bf16[640,1024]{1,0:T(8,128)(2,1)}) %all-gather.23.cloned.1.call-update) | async-done | bytes 1310736 | tf_op jit(solution)/shard_map/all_gather | solution.py:35
  58.9 32.0 %all-gather.39.cloned.1.call-done = bf16[1,1024,3,256]{3,1,2,0:T(8,128)(2,1)} async-done(((bf16[1,256,3,256]{3,1,2,0:T(8,128)(2,1)}), bf16[1,1024,3,256]{3,1,2,0:T(8,128)(2,1)}) %all-gather.39.cloned.1.call-update) | async-done | bytes 1572880 | tf_op jit(solution)/shard_map/all_gather | solution.py:129
  107.8 50.5 %reduce-scatter.17.cloned.1.call-done = f32[640,256]{1,0:T(8,128)} async-done(((f32[640,1024]{1,0:T(8,128)}), f32[640,256]{1,0:T(8,128)}) %reduce-scatter.17.cloned.1.call-update) | async-done | bytes 655376 | tf_op jit(solution)/shard_map/reduce_scatter | solution.py:17
  159.6 10.3 all-reduce.8
  174.1 21.4 %all-gather.41.cloned.1.call-done = bf16[1,1024,1024]{2,1,0:T(8,128)(2,1)} async-done(((bf16[1,256,1024]{2,1,0:T(8,128)(2,1)}), bf16[1,1024,1024]{2,1,0:T(8,128)(2,1)}) %all-gather.41.cloned.1.call-update) | async-done | bytes 2097168 | tf_op jit(solution)/shard_map/all_gather | solution.py:131
  195.5 35.5 %all-gather.25.cloned.1.call-done = bf16[640,1024]{1,0:T(8,128)(2,1)} async-done(((bf16[640,256]{1,0:T(8,128)(2,1)}), bf16[640,1024]{1,0:T(8,128)(2,1)}) %all-gather.25.cloned.1.call-update) | async-done | bytes 1310736 | tf_op jit(solution)/shard_map/all_gather | solution.py:35
  231.0 10.3 multiply_convert_fusion.3
  241.3 25.7 %all-gather.43.cloned.1.call-done = bf16[1,1024,1024]{2,1,0:T(8,128)(2,1)} async-done(((bf16[1,1024,256]{2,1,0:T(8,128)(2,1)}), bf16[1,1024,1024]{2,1,0:T(8,128)(2,1)}) %all-gather.43.cloned.1.call-update) | async-done | bytes 2097168 | tf_op jit(solution)/shard_map/all_gather | solution.py:132
  267.0 5.1 fusion.26
  273.6 50.8 %reduce-scatter.19.cloned.1.call-done = f32[640,256]{1,0:T(8,128)} async-done(((f32[640,1024]{1,0:T(8,128)}), f32[640,256]{1,0:T(8,128)}) %reduce-scatter.19.cloned.1.call-update) | async-done | bytes 655376 | tf_op jit(solution)/shard_map/reduce_scatter | solution.py:17
  325.9 10.3 all-reduce.7
  338.6 16.2 %all-gather.5 = bf16[1,256,1024]{2,1,0:T(8,128)(2,1)} all-gather(bf16[1,256,256]{2,1,0:T(8,128)(2,1)S(1)} %copy-done.32), channel_id=7, replica_groups=mesh['dp'=2,'row'=4,'col'=4] {'row'}, dimensions={2}, use_global_device_ids=true | all-gather | bytes 655360 | tf_op jit(solution)/shard_map/all_gather | solution.py:130
  354.7 5.8 all-gather.45.cloned.1.call-done
  360.5 34.8 %all-gather.27.cloned.1.call-done = bf16[640,1024]{1,0:T(8,128)(2,1)} async-done(((bf16[640,256]{1,0:T(8,128)(2,1)}), bf16[640,1024]{1,0:T(8,128)(2,1)}) %all-gather.27.cloned.1.call-update) | async-done | bytes 1310736 | tf_op jit(solution)/shard_map/all_gather | solution.py:35
  422.2 50.0 %reduce-scatter.21.cloned.1.call-done = f32[640,256]{1,0:T(8,128)} async-done(((f32[640,1024]{1,0:T(8,128)}), f32[640,256]{1,0:T(8,128)}) %reduce-scatter.21.cloned.1.call-update) | async-done | bytes 655376 | tf_op jit(solution)/shard_map/reduce_scatter | solution.py:17
  473.6 10.3 all-reduce.6
  486.1 23.5 %all-gather.47.cloned.1.call-done = bf16[1,1024,1024]{2,1,0:T(8,128)(2,1)} async-done(((bf16[1,256,1024]{2,1,0:T(8,128)(2,1)}), bf16[1,1024,1024]{2,1,0:T(8,128)(2,1)}) %all-gather.47.cloned.1.call-update) | async-done | bytes 2097168 | tf_op jit(solution)/shard_map/all_gather | solution.py:131
  509.7 35.5 %all-gather.29.cloned.1.call-done = bf16[640,1024]{1,0:T(8,128)(2,1)} async-done(((bf16[640,256]{1,0:T(8,128)(2,1)}), bf16[640,1024]{1,0:T(8,128)(2,1)}) %all-gather.29.cloned.1.call-update) | async-done | bytes 1310736 | tf_op jit(solution)/shard_map/all_gather | solution.py:35
  545.1 10.3 multiply_convert_fusion.2
  555.4 25.9 %all-gather.49.cloned.1.call-done = bf16[1,1024,1024]{2,1,0:T(8,128)(2,1)} async-done(((bf16[1,1024,256]{2,1,0:T(8,128)(2,1)}), bf16[1,1024,1024]{2,1,0:T(8,128)(2,1)}) %all-gather.49.cloned.1.call-update) | async-done | bytes 2097168 | tf_op jit(solution)/shard_map/all_gather | solution.py:132
  588.2 50.3 %reduce-scatter.23.cloned.1.call-done = f32[640,256]{1,0:T(8,128)} async-done(((f32[640,1024]{1,0:T(8,128)}), f32[640,256]{1,0:T(8,128)}) %reduce-scatter.23.cloned.1.call-update) | async-done | bytes 655376 | tf_op jit(solution)/shard_map/reduce_scatter | solution.py:17
  641.4 40.1 %all-reduce = (f32[]{:T(128)}, f32[]{:T(128)}) all-reduce(f32[]{:T(128)} %get-tuple-element.90, f32[]{:T(128)S(6)} %select_n.15), channel_id=1, replica_groups=mesh['dp'=2,'row'=4,'col'=4] {'dp','row','col'}, use_global_device_ids=true, to_apply=%region_25.26 | all-reduce | flops 2 | bytes 16 | tf_op jit(solution)/shard_map/psum | solution.py:183
  684.6 33.5 %all-gather.31.cloned.1.call-done = bf16[640,1024]{1,0:T(8,128)(2,1)} async-done(((bf16[640,256]{1,0:T(8,128)(2,1)}), bf16[640,1024]{1,0:T(8,128)(2,1)}) %all-gather.31.cloned.1.call-update) | async-done | bytes 1310736 | tf_op jit(solution)/shard_map/all_gather | solution.py:27
  718.1 6.1 convert_reduce_fusion
  727.9 29.8 %reduce-scatter.25.cloned.1.call-done = bf16[640,256]{1,0:T(8,128)(2,1)} async-done(((bf16[640,1024]{1,0:T(8,128)(2,1)}), bf16[640,256]{1,0:T(8,128)(2,1)}) %reduce-scatter.25.cloned.1.call-update) | async-done | bytes 327696 | tf_op jit(solution)/shard_map/reduce_scatter | solution.py:21
  759.2 9.7 all-reduce.5
  772.1 31.7 %all-gather.33.cloned.1.call-done = bf16[640,1024]{1,0:T(8,128)(2,1)} async-done(((bf16[640,256]{1,0:T(8,128)(2,1)}), bf16[640,1024]{1,0:T(8,128)(2,1)}) %all-gather.33.cloned.1.call-update) | async-done | bytes 1310736 | tf_op jit(solution)/shard_map/all_gather | solution.py:27
  831.2 29.9 %reduce-scatter.27.cloned.1.call-done = bf16[640,256]{1,0:T(8,128)(2,1)} async-done(((bf16[640,1024]{1,0:T(8,128)(2,1)}), bf16[640,256]{1,0:T(8,128)(2,1)}) %reduce-scatter.27.cloned.1.call-update) | async-done | bytes 327696 | tf_op jit(solution)/shard_map/reduce_scatter | solution.py:21
  862.5 9.7 all-reduce.4
  875.0 31.7 %all-gather.35.cloned.1.call-done = bf16[640,1024]{1,0:T(8,128)(2,1)} async-done(((bf16[640,256]{1,0:T(8,128)(2,1)}), bf16[640,1024]{1,0:T(8,128)(2,1)}) %all-gather.35.cloned.1.call-update) | async-done | bytes 1310736 | tf_op jit(solution)/shard_map/all_gather | solution.py:27
  906.7 6.1 convert_reduce_fusion.1
  916.6 29.9 %reduce-scatter.29.cloned.1.call-done = bf16[640,256]{1,0:T(8,128)(2,1)} async-done(((bf16[640,1024]{1,0:T(8,128)(2,1)}), bf16[640,256]{1,0:T(8,128)(2,1)}) %reduce-scatter.29.cloned.1.call-update) | async-done | bytes 327696 | tf_op jit(solution)/shard_map/reduce_scatter | solution.py:21
  947.9 9.7 all-reduce.3
  965.0 5.1 convolution_convert_fusion.2
  975.8 5.0 convolution_convert_fusion.1
  985.7 6.3 all-gather.37.cloned.1.call-done
  1028.7 39.0 %reduce-scatter.43.cloned.1.call-done = bf16[256,1024]{1,0:T(8,128)(2,1)} async-done(((bf16[1024,1024]{1,0:T(8,128)(2,1)}), bf16[256,1024]{1,0:T(8,128)(2,1)}) %reduce-scatter.43.cloned.1.call-update) | async-done | bytes 524304 | tf_op jit(solution)/shard_map/reduce_scatter | solution.py:278
  1067.8 28.1 %reduce-scatter.39.cloned.1.call-done = bf16[256,256]{1,0:T(8,128)(2,1)} async-done(((bf16[256,1024]{1,0:T(8,128)(2,1)}), bf16[256,256]{1,0:T(8,128)(2,1)}) %reduce-scatter.39.cloned.1.call-update) | async-done | bytes 131088 | tf_op jit(solution)/shard_map/reduce_scatter | solution.py:275
  1095.8 34.8 %reduce-scatter.35.cloned.1.call-done = bf16[256,3,256]{2,0,1:T(8,128)(2,1)} async-done(((bf16[1024,3,256]{2,0,1:T(8,128)(2,1)}), bf16[256,3,256]{2,0,1:T(8,128)(2,1)}) %reduce-scatter.35.cloned.1.call-update) | async-done | bytes 393232 | tf_op jit(solution)/shard_map/reduce_scatter | solution.py:272
  1130.6 38.3 %reduce-scatter.45.cloned.1.call-done = bf16[1024,256]{1,0:T(8,128)(2,1)} async-done(((bf16[1024,1024]{1,0:T(8,128)(2,1)}), bf16[1024,256]{1,0:T(8,128)(2,1)}) %reduce-scatter.45.cloned.1.call-update) | async-done | bytes 524304 | tf_op jit(solution)/shard_map/reduce_scatter | solution.py:281
  1168.9 38.6 %reduce-scatter.41.cloned.1.call-done = bf16[256,1024]{1,0:T(8,128)(2,1)} async-done(((bf16[1024,1024]{1,0:T(8,128)(2,1)}), bf16[256,1024]{1,0:T(8,128)(2,1)}) %reduce-scatter.41.cloned.1.call-update) | async-done | bytes 524304 | tf_op jit(solution)/shard_map/reduce_scatter | solution.py:278
  1207.5 27.9 %reduce-scatter.37.cloned.1.call-done = bf16[256,256]{1,0:T(8,128)(2,1)} async-done(((bf16[256,1024]{1,0:T(8,128)(2,1)}), bf16[256,256]{1,0:T(8,128)(2,1)}) %reduce-scatter.37.cloned.1.call-update) | async-done | bytes 131088 | tf_op jit(solution)/shard_map/reduce_scatter | solution.py:275
  1235.4 34.0 %reduce-scatter.33.cloned.1.call-done = bf16[256,3,256]{2,0,1:T(8,128)(2,1)} async-done(((bf16[1024,3,256]{2,0,1:T(8,128)(2,1)}), bf16[256,3,256]{2,0,1:T(8,128)(2,1)}) %reduce-scatter.33.cloned.1.call-update) | async-done | bytes 393232 | tf_op jit(solution)/shard_map/reduce_scatter | solution.py:272
  1271.3 31.4 %reduce-scatter.31.cloned.1.call-done = bf16[640,256]{1,0:T(8,128)(2,1)} async-done(((bf16[640,1024]{1,0:T(8,128)(2,1)}), bf16[640,256]{1,0:T(8,128)(2,1)}) %reduce-scatter.31.cloned.1.call-update) | async-done | bytes 327696 | tf_op jit(solution)/shard_map/reduce_scatter | solution.py:21
  1304.2 26.5 %all-reduce.1 = (f32[1,2,256]{2,1,0:T(2,128)S(1)}, f32[1,2,256]{2,1,0:T(2,128)S(1)}, f32[1,2,256]{2,1,0:T(2,128)S(1)}, f32[1,2,256]{2,1,0:T(2,128)S(1)}, f32[1,2...) all-reduce(f32[1,2,256]{2,1,0:T(2,128)S(1)} %maximum_bitcast_fusion, ...), channel_id=1, replica_groups=mesh['dp'=2,'row'=4,'col'=4] {'dp','row'}, use_global_device_ids=true, to_apply=%region_55.56 | all-reduce | flops 6144 | bytes 49152 | tf_op jit(solution)/shard_map/psum | solution.py:291
  1330.7 9.7 all-reduce.2
  (394 shorter events, 192.6 us)
Async XLA Ops:
  7.2 51.7 %all-gather.23.cloned.1.call-start = ((), (), s32[]{:S(2)}) async-start(), calls=%async_computation.16 | async-start | bytes 1638400 | tf_op jit(solution)/shard_map/all_gather | solution.py:35
  27.1 63.8 %all-gather.39.cloned.1.call-start = ((), (), s32[]{:S(2)}) async-start(), calls=%async_computation.40 | async-start | bytes 1966080 | tf_op jit(solution)/shard_map/all_gather | solution.py:129
  29.2 129.1 %reduce-scatter.17.cloned.1.call-start = ((), (), s32[]{:S(2)}) async-start(), calls=%async_computation.17 | async-start | bytes 3276800 | tf_op jit(solution)/shard_map/reduce_scatter | solution.py:17
  29.9 69.5 %copy-start.63 = (f32[4,64]{1,0:T(4,128)}, f32[4,64]{1,0:T(4,128)S(1)}, u32[]{:S(2)}) copy-start(f32[4,64]{1,0:T(4,128)S(1)} %add.318) | copy-start | bytes 3076
  30.0 71.1 %copy-start.59 = (f32[4,64]{1,0:T(4,128)}, f32[4,64]{1,0:T(4,128)S(1)}, u32[]{:S(2)}) copy-start(f32[4,64]{1,0:T(4,128)S(1)} %add.315) | copy-start | bytes 3076
  106.0 89.5 %all-gather.41.cloned.1.call-start = ((), (), s32[]{:S(2)}) async-start(), calls=%async_computation.41 | async-start | bytes 2621440 | tf_op jit(solution)/shard_map/all_gather | solution.py:131
  107.1 123.9 %all-gather.25.cloned.1.call-start = ((), (), s32[]{:S(2)}) async-start(), calls=%async_computation.18 | async-start | bytes 1638400 | tf_op jit(solution)/shard_map/all_gather | solution.py:35
  169.9 71.4 %copy-start.47 = (f32[640]{0:T(1024)}, f32[640]{0:T(1024)S(1)}, u32[]{:S(2)}) copy-start(f32[640]{0:T(1024)S(1)} %get-tuple-element.125) | copy-start | bytes 7684
  169.9 71.4 %copy-start.49 = (f32[640]{0:T(1024)}, f32[640]{0:T(1024)S(1)}, u32[]{:S(2)}) copy-start(f32[640]{0:T(1024)S(1)} %get-tuple-element.126) | copy-start | bytes 7684
  170.9 96.1 %all-gather.43.cloned.1.call-start = ((), (), s32[]{:S(2)}) async-start(), calls=%async_computation.42 | async-start | bytes 2621440 | tf_op jit(solution)/shard_map/all_gather | solution.py:132
  173.2 151.2 %reduce-scatter.19.cloned.1.call-start = ((), (), s32[]{:S(2)}) async-start(), calls=%async_computation.19 | async-start | bytes 3276800 | tf_op jit(solution)/shard_map/reduce_scatter | solution.py:17
  174.1 67.2 %copy-start.79 = (f32[1,1024]{1,0:T(1,128)}, f32[1,1024]{1,0:T(1,128)S(1)}, u32[]{:S(2)}) copy-start(f32[1,1024]{1,0:T(1,128)S(1)} %get-tuple-element.112) | copy-start | bytes 12292
  272.1 65.8 %copy-start.82 = (f32[256]{0:T(256)S(1)}, f32[256]{0:T(256)}, u32[]{:S(2)}) copy-start(f32[256]{0:T(256)} %get-tuple-element.40) | copy-start | bytes 3076
  272.1 66.5 %copy-start.32 = (bf16[1,256,256]{2,1,0:T(8,128)(2,1)S(1)}, bf16[1,256,256]{2,1,0:T(8,128)(2,1)}, u32[]{:S(2)}) copy-start(bf16[1,256,256]{2,1,0:T(8,128)(2,1)} %get-tuple-element.109) | copy-start | bytes 393220
  272.1 88.4 %all-gather.45.cloned.1.call-start = ((), (), s32[]{:S(2)}) async-start(), calls=%async_computation.43 | async-start | bytes 1966080 | tf_op jit(solution)/shard_map/all_gather | solution.py:129
  272.9 122.4 %all-gather.27.cloned.1.call-start = ((), (), s32[]{:S(2)}) async-start(), calls=%async_computation.20 | async-start | bytes 1638400 | tf_op jit(solution)/shard_map/all_gather | solution.py:35
  337.2 135.0 %reduce-scatter.21.cloned.1.call-start = ((), (), s32[]{:S(2)}) async-start(), calls=%async_computation.21 | async-start | bytes 3276800 | tf_op jit(solution)/shard_map/reduce_scatter | solution.py:17
  421.4 123.7 %copy-start.81 = (f32[1,1024]{1,0:T(1,128)S(1)}, f32[1,1024]{1,0:T(1,128)}, u32[]{:S(2)}) copy-start(f32[1,1024]{1,0:T(1,128)} %get-tuple-element.111) | copy-start | bytes 12292
  421.4 88.2 %all-gather.47.cloned.1.call-start = ((), (), s32[]{:S(2)}) async-start(), calls=%async_computation.44 | async-start | bytes 2621440 | tf_op jit(solution)/shard_map/all_gather | solution.py:131
  422.2 123.0 %all-gather.29.cloned.1.call-start = ((), (), s32[]{:S(2)}) async-start(), calls=%async_computation.22 | async-start | bytes 1638400 | tf_op jit(solution)/shard_map/all_gather | solution.py:35
  484.9 96.4 %all-gather.49.cloned.1.call-start = ((), (), s32[]{:S(2)}) async-start(), calls=%async_computation.45 | async-start | bytes 2621440 | tf_op jit(solution)/shard_map/all_gather | solution.py:132
  485.6 152.9 %reduce-scatter.23.cloned.1.call-start = ((), (), s32[]{:S(2)}) async-start(), calls=%async_computation.23 | async-start | bytes 3276800 | tf_op jit(solution)/shard_map/reduce_scatter | solution.py:17
  586.2 131.8 %all-gather.31.cloned.1.call-start = ((), (), s32[]{:S(2)}) async-start(), calls=%async_computation.24 | async-start | bytes 1638400 | tf_op jit(solution)/shard_map/all_gather | solution.py:27
  684.5 73.3 %reduce-scatter.25.cloned.1.call-start = ((), (), s32[]{:S(2)}) async-start(), calls=%async_computation.25 | async-start | bytes 1638400 | tf_op jit(solution)/shard_map/reduce_scatter | solution.py:21
  727.9 76.0 %all-gather.33.cloned.1.call-start = ((), (), s32[]{:S(2)}) async-start(), calls=%async_computation.26 | async-start | bytes 1638400 | tf_op jit(solution)/shard_map/all_gather | solution.py:27
  771.8 89.3 %reduce-scatter.27.cloned.1.call-start = ((), (), s32[]{:S(2)}) async-start(), calls=%async_computation.27 | async-start | bytes 1638400 | tf_op jit(solution)/shard_map/reduce_scatter | solution.py:21
  831.1 75.6 %copy-start.80 = (f32[1,1024]{1,0:T(1,128)S(1)}, f32[1,1024]{1,0:T(1,128)}, u32[]{:S(2)}) copy-start(f32[1,1024]{1,0:T(1,128)} %copy-done.79) | copy-start | bytes 12292
  831.2 75.5 %all-gather.35.cloned.1.call-start = ((), (), s32[]{:S(2)}) async-start(), calls=%async_computation.28 | async-start | bytes 1638400 | tf_op jit(solution)/shard_map/all_gather | solution.py:27
  874.7 71.8 %reduce-scatter.29.cloned.1.call-start = ((), (), s32[]{:S(2)}) async-start(), calls=%async_computation.29 | async-start | bytes 1638400 | tf_op jit(solution)/shard_map/reduce_scatter | solution.py:21
  916.5 75.5 %all-gather.37.cloned.1.call-start = ((), (), s32[]{:S(2)}) async-start(), calls=%async_computation.30 | async-start | bytes 1638400 | tf_op jit(solution)/shard_map/all_gather | solution.py:27
  960.0 68.7 %reduce-scatter.47.cloned.1.call-start = ((), (), s32[]{:S(2)}) async-start(), calls=%async_computation.39 | async-start | bytes 2621440 | tf_op jit(solution)/shard_map/reduce_scatter | solution.py:281
  965.0 102.8 %reduce-scatter.43.cloned.1.call-start = ((), (), s32[]{:S(2)}) async-start(), calls=%async_computation.37 | async-start | bytes 2621440 | tf_op jit(solution)/shard_map/reduce_scatter | solution.py:278
  970.1 125.7 %reduce-scatter.39.cloned.1.call-start = ((), (), s32[]{:S(2)}) async-start(), calls=%async_computation.35 | async-start | bytes 655360 | tf_op jit(solution)/shard_map/reduce_scatter | solution.py:275
  971.6 159.0 %reduce-scatter.35.cloned.1.call-start = ((), (), s32[]{:S(2)}) async-start(), calls=%async_computation.33 | async-start | bytes 1966080 | tf_op jit(solution)/shard_map/reduce_scatter | solution.py:272
  975.7 193.2 %reduce-scatter.45.cloned.1.call-start = ((), (), s32[]{:S(2)}) async-start(), calls=%async_computation.38 | async-start | bytes 2621440 | tf_op jit(solution)/shard_map/reduce_scatter | solution.py:281
  980.8 226.7 %reduce-scatter.41.cloned.1.call-start = ((), (), s32[]{:S(2)}) async-start(), calls=%async_computation.36 | async-start | bytes 2621440 | tf_op jit(solution)/shard_map/reduce_scatter | solution.py:278
  985.6 249.7 %reduce-scatter.37.cloned.1.call-start = ((), (), s32[]{:S(2)}) async-start(), calls=%async_computation.34 | async-start | bytes 655360 | tf_op jit(solution)/shard_map/reduce_scatter | solution.py:275
  999.4 270.0 %reduce-scatter.33.cloned.1.call-start = ((), (), s32[]{:S(2)}) async-start(), calls=%async_computation.32 | async-start | bytes 1966080 | tf_op jit(solution)/shard_map/reduce_scatter | solution.py:272
  1023.9 278.8 %reduce-scatter.31.cloned.1.call-start = ((), (), s32[]{:S(2)}) async-start(), calls=%async_computation.31 | async-start | bytes 1638400 | tf_op jit(solution)/shard_map/reduce_scatter | solution.py:21
  1026.3 244.4 %copy-start.16 = (bf16[640,1,256]{0,2,1:T(8,128)(2,1)S(1)}, bf16[640,1,256]{0,2,1:T(8,128)(2,1)}, u32[]{:S(2)}) copy-start(bf16[640,1,256]{0,2,1:T(8,128)(2,1)} %copy-done.15) | copy-start | bytes 983044
  1026.3 244.6 %copy-start.18 = (bf16[640,1,256]{0,2,1:T(8,128)(2,1)S(1)}, bf16[640,1,256]{0,2,1:T(8,128)(2,1)}, u32[]{:S(2)}) copy-start(bf16[640,1,256]{0,2,1:T(8,128)(2,1)} %copy-done.17) | copy-start | bytes 983044
  1026.3 244.7 %copy-start.19 = (bf16[640,1,256]{0,2,1:T(8,128)(2,1)S(1)}, bf16[640,1,256]{0,2,1:T(8,128)(2,1)}, u32[]{:S(2)}) copy-start(bf16[640,1,256]{0,2,1:T(8,128)(2,1)} %stack_reshape.29) | copy-start | bytes 983044
  1026.3 244.9 %copy-start.20 = (bf16[640,1,256]{0,2,1:T(8,128)(2,1)S(1)}, bf16[640,1,256]{0,2,1:T(8,128)(2,1)}, u32[]{:S(2)}) copy-start(bf16[640,1,256]{0,2,1:T(8,128)(2,1)} %stack_reshape.27) | copy-start | bytes 983044
  1026.3 276.4 %copy-start.44 = (f32[640]{0:T(1024)S(1)}, f32[640]{0:T(1024)}, u32[]{:S(2)}) copy-start(f32[640]{0:T(1024)} %copy-done.43) | copy-start | bytes 7684
  1026.3 276.4 %copy-start.46 = (f32[640]{0:T(1024)S(1)}, f32[640]{0:T(1024)}, u32[]{:S(2)}) copy-start(f32[640]{0:T(1024)} %copy-done.45) | copy-start | bytes 7684
  1026.3 276.4 %copy-start.67 = (f32[1,1,256]{2,1,0:T(1,128)S(1)}, f32[1,1,256]{2,1,0:T(1,128)}, u32[]{:S(2)}) copy-start(f32[1,1,256]{2,1,0:T(1,128)} %copy-done.66) | copy-start | bytes 3076
  1026.3 318.6 %all-reduce.13.cloned.1.call-start = ((), (), s32[]{:S(2)}) async-start(), calls=%async_computation.46 | async-start | bytes 6291456 | tf_op jit(solution)/shard_map/psum | solution.py:286
  1269.3 73.4 %copy-start.25 = (f32[640,256]{1,0:T(8,128)S(1)}, f32[640,256]{1,0:T(8,128)}, u32[]{:S(2)}) copy-start(f32[640,256]{1,0:T(8,128)} %get-tuple-element.86) | copy-start | bytes 1966084
  (80 other events, 1475.5 us)
Sparse Core Ops, SparseCore 0:
  27.2 31.6 all-gather.22
  61.3 29.4 all-gather.38
  106.1 52.0 reduce-scatter.16
  160.5 34.9 all-gather.40
  197.5 33.4 all-gather.24
  233.2 33.6 all-gather.42
  272.2 52.1 reduce-scatter.18
  326.8 33.6 all-gather.44
  362.6 32.5 all-gather.26
  421.5 50.6 reduce-scatter.20
  474.6 34.9 all-gather.46
  511.6 33.4 all-gather.28
  547.5 33.6 all-gather.48
  586.4 52.0 reduce-scatter.22
  684.6 33.3 all-gather.30
  728.0 29.7 reduce-scatter.24
  772.0 31.8 all-gather.32
  831.3 29.7 reduce-scatter.26
  874.8 31.8 all-gather.34
  916.6 29.7 reduce-scatter.28
  960.1 31.8 all-gather.36
  995.0 33.7 reduce-scatter.46
  1032.5 35.1 reduce-scatter.42
  1071.0 24.7 reduce-scatter.38
  1099.7 30.9 reduce-scatter.34
  1133.7 35.1 reduce-scatter.44
  1172.3 35.1 reduce-scatter.40
  1210.5 24.7 reduce-scatter.36
  1238.4 30.9 reduce-scatter.32
  1271.5 31.2 reduce-scatter.30
  1305.6 22.3 all-reduce.12
where the time goes:
time: 1370 us; the launch traced here: 1360 us
  waiting for transfers between devices  926 us (68%)
  blocking collectives  179 us (13%)
  matrix products  120 us (9%)
  local copies, waits for them, and re-layouts  67.1 us (5%)
  other arithmetic  45.5 us (3%)
  between operations  20.2 us (1%)
    reduce_scatter x4, waiting for transfers between devices, feature_rows(): lax.psum_scatter(partial_value, 'col', scatter_dimension=1, tiled=True)  202 us
    reduce_scatter x4, waiting for transfers between devices, gradient_rows(): lax.psum_scatter(partial_value.astype(jnp.bfloat16), 'col', scatter_dimen...  121 us
    all_gather x4, waiting for transfers between devices, norm_shares(): lax.all_gather((standard * gains + shifts).astype(jnp.bfloat16), 'col', a...  120 us
    all_gather x4, waiting for transfers between devices, gather_gradient(): return lax.all_gather(gradient, 'col', axis=1, tiled=True)  103 us
    reduce_scatter x2, waiting for transfers between devices, body(): lax.psum_scatter(up_part.astype(jnp.bfloat16), 'row', scatter_dimension=0...  77.6 us
    reduce_scatter x2, waiting for transfers between devices, body(): lax.psum_scatter(in_part.astype(jnp.bfloat16), 'row', scatter_dimension=0...  68.7 us
    reduce_scatter x2, waiting for transfers between devices, body(): lax.psum_scatter(proj_part.astype(jnp.bfloat16), 'row', scatter_dimension...  55.9 us
    all_gather x2, waiting for transfers between devices, body(): lax.all_gather(down_weight[layer_index], 'row', axis=1, tiled=True)  51.6 us
  transfers between devices with their start and end apart: 31, of which 30 were waited for; matrix products, arithmetic and copies ran while one was open for 8% of the time, Pallas kernels for 0%

commit v1 on v0

--- a/solution.py
+++ b/solution.py
@@ -9,6 +9,17 @@
 fill_value = -1e30
 
 
+def ring_gather(x, axis, dim):
+    ways = lax.axis_size(axis)
+    pieces = [x]
+    for far in range(1, ways):
+        pieces.append(
+            lax.ppermute(pieces[far - 1], axis, [(d, (d - 1) % ways) for d in range(ways)])
+        )
+    line = jnp.concatenate(pieces, axis=dim)
+    return jnp.roll(line, lax.axis_index(axis) * x.shape[dim], axis=dim)
+
+
 def gelu_exact(inputs):
     return jax.nn.gelu(inputs, approximate=False)
 
@@ -24,7 +35,7 @@
 
 
 def gather_gradient(gradient):
-    return lax.all_gather(gradient, "col", axis=1, tiled=True)
+    return ring_gather(gradient, "col", 1)
 
 
 def norm_shares(inputs, gains, shifts, model_width):

time: 1370 us -> 1320 us (0.964)
  waiting for transfers between devices: 926 us -> 843 us
  starting transfers between devices: 2.89 us -> 28.8 us
    all_gather x4 -> x0, waiting for transfers between devices: 103 us -> none  [gather_gradient(): return lax.all_gather(gradient, 'col', axis=1, tiled=True)]
    ppermute x0 -> x12, waiting for transfers between devices: none -> 71.9 us  [ring_gather(): lax.ppermute(pieces[far - 1], axis, [(d, (d - 1) % ways) for d in range(w...]
    reduce_scatter x2, waiting for transfers between devices: 77.6 us -> 39.8 us  [body(): lax.psum_scatter(up_part.astype(jnp.bfloat16), 'row', scatter_dimension=0...]
    ppermute x0 -> x12, starting transfers between devices: none -> 26.8 us  [ring_gather(): lax.ppermute(pieces[far - 1], axis, [(d, (d - 1) % ways) for d in range(w...]
    reduce_scatter x4, waiting for transfers between devices: 121 us -> 104 us  [gradient_rows(): lax.psum_scatter(partial_value.astype(jnp.bfloat16), 'col', scatter_dimen...]
  transfers between devices with their start and end apart: 31 -> 39, of which waited for: 30 -> 37; matrix products, arithmetic and copies ran while one was open for 8% -> 8% of each run, Pallas kernels for 0% -> 0%
where the time goes in v1:
time: 1320 us; the launch traced here: 1310 us
  waiting for transfers between devices  843 us (64%)
  blocking collectives  176 us (13%)
  matrix products  119 us (9%)
  local copies, waits for them, and re-layouts  69 us (5%)
  other arithmetic  52.8 us (4%)
  starting transfers between devices  28.8 us (2%)
  between operations  20.1 us (2%)
    reduce_scatter x4, waiting for transfers between devices, feature_rows(): lax.psum_scatter(partial_value, 'col', scatter_dimension=1, tiled=True)  202 us
    all_gather x4, waiting for transfers between devices, norm_shares(): lax.all_gather((standard * gains + shifts).astype(jnp.bfloat16), 'col', a...  121 us
    reduce_scatter x4, waiting for transfers between devices, gradient_rows(): lax.psum_scatter(partial_value.astype(jnp.bfloat16), 'col', scatter_dimen...  104 us
    ppermute x12, waiting for transfers between devices, ring_gather(): lax.ppermute(pieces[far - 1], axis, [(d, (d - 1) % ways) for d in range(w...  71.9 us
    reduce_scatter x2, waiting for transfers between devices, body(): lax.psum_scatter(in_part.astype(jnp.bfloat16), 'row', scatter_dimension=0...  68.7 us
    reduce_scatter x2, waiting for transfers between devices, body(): lax.psum_scatter(proj_part.astype(jnp.bfloat16), 'row', scatter_dimension...  55.8 us
    all_gather x2, waiting for transfers between devices, body(): lax.all_gather(down_weight[layer_index], 'row', axis=1, tiled=True)  51 us
    all_gather x2, waiting for transfers between devices, body(): lax.all_gather(up_weight[layer_index], 'row', axis=0, tiled=True)  46.2 us
  transfers between devices with their start and end apart: 39, of which 37 were waited for; matrix products, arithmetic and copies ran while one was open for 8% of the time, Pallas kernels for 0%

profile of v1, /device:TPU:0, one launch (start us, length us, event | category | flops | bytes accessed | tf_op | source)
XLA Modules:
  0.0 1308.5 jit_solution(14883557801642936767)
XLA Ops:
  11.3 13.7 %all-reduce.9 = (f32[640]{0:T(1024)S(1)}, f32[640]{0:T(1024)S(1)}) all-reduce(f32[640]{0:T(1024)S(1)} %get-tuple-element.29, f32[640]{0:T(1024)S(1)} %get-tuple-element.28), channel_id=1, replica_groups=mesh['dp'=2,'row'=4,'col'=4] {'col'}, use_global_device_ids=true, to_apply=%region_3.0 | all-reduce | flops 1280 | bytes 10240 | tf_op jit(solution)/shard_map/psum | solution.py:42
  31.3 12.9 all-gather.1
  44.8 14.7 %all-gather.19.cloned.1.call-done = bf16[640,1024]{1,0:T(8,128)(2,1)} async-done(((bf16[640,256]{1,0:T(8,128)(2,1)}), bf16[640,1024]{1,0:T(8,128)(2,1)}) %all-gather.19.cloned.1.call-update) | async-done | bytes 1310736 | tf_op jit(solution)/shard_map/all_gather | solution.py:46
  59.5 32.0 %all-gather.27.cloned.1.call-done = bf16[1,1024,3,256]{3,1,2,0:T(8,128)(2,1)} async-done(((bf16[1,256,3,256]{3,1,2,0:T(8,128)(2,1)}), bf16[1,1024,3,256]{3,1,2,0:T(8,128)(2,1)}) %all-gather.27.cloned.1.call-update) | async-done | bytes 1572880 | tf_op jit(solution)/shard_map/all_gather | solution.py:140
  106.1 50.5 %reduce-scatter.17.cloned.1.call-done = f32[640,256]{1,0:T(8,128)} async-done(((f32[640,1024]{1,0:T(8,128)}), f32[640,256]{1,0:T(8,128)}) %reduce-scatter.17.cloned.1.call-update) | async-done | bytes 655376 | tf_op jit(solution)/shard_map/reduce_scatter | solution.py:28
  158.0 10.2 all-reduce.8
  171.5 22.4 %all-gather.29.cloned.1.call-done = bf16[1,1024,1024]{2,1,0:T(8,128)(2,1)} async-done(((bf16[1,256,1024]{2,1,0:T(8,128)(2,1)}), bf16[1,1024,1024]{2,1,0:T(8,128)(2,1)}) %all-gather.29.cloned.1.call-update) | async-done | bytes 2097168 | tf_op jit(solution)/shard_map/all_gather | solution.py:142
  193.9 35.5 %all-gather.21.cloned.1.call-done = bf16[640,1024]{1,0:T(8,128)(2,1)} async-done(((bf16[640,256]{1,0:T(8,128)(2,1)}), bf16[640,1024]{1,0:T(8,128)(2,1)}) %all-gather.21.cloned.1.call-update) | async-done | bytes 1310736 | tf_op jit(solution)/shard_map/all_gather | solution.py:46
  229.4 10.3 multiply_convert_fusion.3
  239.7 25.7 %all-gather.31.cloned.1.call-done = bf16[1,1024,1024]{2,1,0:T(8,128)(2,1)} async-done(((bf16[1,1024,256]{2,1,0:T(8,128)(2,1)}), bf16[1,1024,1024]{2,1,0:T(8,128)(2,1)}) %all-gather.31.cloned.1.call-update) | async-done | bytes 2097168 | tf_op jit(solution)/shard_map/all_gather | solution.py:143
  265.4 5.1 fusion.26
  271.9 50.9 %reduce-scatter.19.cloned.1.call-done = f32[640,256]{1,0:T(8,128)} async-done(((f32[640,1024]{1,0:T(8,128)}), f32[640,256]{1,0:T(8,128)}) %reduce-scatter.19.cloned.1.call-update) | async-done | bytes 655376 | tf_op jit(solution)/shard_map/reduce_scatter | solution.py:28
  324.2 10.3 all-reduce.7
  335.8 13.3 %all-gather.5 = bf16[1,256,1024]{2,1,0:T(8,128)(2,1)} all-gather(bf16[1,256,256]{2,1,0:T(8,128)(2,1)S(1)} %get-tuple-element.110), channel_id=7, replica_groups=mesh['dp'=2,'row'=4,'col'=4] {'row'}, dimensions={2}, use_global_device_ids=true | all-gather | bytes 655360 | tf_op jit(solution)/shard_map/all_gather | solution.py:141
  349.1 9.4 all-gather.33.cloned.1.call-done
  358.5 35.6 %all-gather.23.cloned.1.call-done = bf16[640,1024]{1,0:T(8,128)(2,1)} async-done(((bf16[640,256]{1,0:T(8,128)(2,1)}), bf16[640,1024]{1,0:T(8,128)(2,1)}) %all-gather.23.cloned.1.call-update) | async-done | bytes 1310736 | tf_op jit(solution)/shard_map/all_gather | solution.py:46
  422.4 50.0 %reduce-scatter.21.cloned.1.call-done = f32[640,256]{1,0:T(8,128)} async-done(((f32[640,1024]{1,0:T(8,128)}), f32[640,256]{1,0:T(8,128)}) %reduce-scatter.21.cloned.1.call-update) | async-done | bytes 655376 | tf_op jit(solution)/shard_map/reduce_scatter | solution.py:28
  473.7 10.3 all-reduce.6
  486.0 23.8 %all-gather.35.cloned.1.call-done = bf16[1,1024,1024]{2,1,0:T(8,128)(2,1)} async-done(((bf16[1,256,1024]{2,1,0:T(8,128)(2,1)}), bf16[1,1024,1024]{2,1,0:T(8,128)(2,1)}) %all-gather.35.cloned.1.call-update) | async-done | bytes 2097168 | tf_op jit(solution)/shard_map/all_gather | solution.py:142
  509.8 35.5 %all-gather.25.cloned.1.call-done = bf16[640,1024]{1,0:T(8,128)(2,1)} async-done(((bf16[640,256]{1,0:T(8,128)(2,1)}), bf16[640,1024]{1,0:T(8,128)(2,1)}) %all-gather.25.cloned.1.call-update) | async-done | bytes 1310736 | tf_op jit(solution)/shard_map/all_gather | solution.py:46
  545.3 10.3 multiply_convert_fusion.2
  555.6 25.3 %all-gather.37.cloned.1.call-done = bf16[1,1024,1024]{2,1,0:T(8,128)(2,1)} async-done(((bf16[1,1024,256]{2,1,0:T(8,128)(2,1)}), bf16[1,1024,1024]{2,1,0:T(8,128)(2,1)}) %all-gather.37.cloned.1.call-update) | async-done | bytes 2097168 | tf_op jit(solution)/shard_map/all_gather | solution.py:143
  587.8 50.3 %reduce-scatter.23.cloned.1.call-done = f32[640,256]{1,0:T(8,128)} async-done(((f32[640,1024]{1,0:T(8,128)}), f32[640,256]{1,0:T(8,128)}) %reduce-scatter.23.cloned.1.call-update) | async-done | bytes 655376 | tf_op jit(solution)/shard_map/reduce_scatter | solution.py:28
  641.0 40.1 %all-reduce = (f32[]{:T(128)}, f32[]{:T(128)}) all-reduce(f32[]{:T(128)} %get-tuple-element.91, f32[]{:T(128)S(6)} %select_n.25), channel_id=1, replica_groups=mesh['dp'=2,'row'=4,'col'=4] {'dp','row','col'}, use_global_device_ids=true, to_apply=%region_25.26 | all-reduce | flops 2 | bytes 16 | tf_op jit(solution)/shard_map/psum | solution.py:194
  686.4 6.5 collective-permute-done
  697.7 5.4 collective-permute-done.1
  715.4 5.5 convert_reduce_fusion
  724.7 32.9 %reduce-scatter.25.cloned.1.call-done = bf16[640,256]{1,0:T(8,128)(2,1)} async-done(((bf16[640,1024]{1,0:T(8,128)(2,1)}), bf16[640,256]{1,0:T(8,128)(2,1)}) %reduce-scatter.25.cloned.1.call-update) | async-done | bytes 327696 | tf_op jit(solution)/shard_map/reduce_scatter | solution.py:32
  759.0 9.7 all-reduce.5
  772.8 7.1 collective-permute-done.3
  781.9 6.7 collective-permute-done.4
  826.1 32.9 %reduce-scatter.27.cloned.1.call-done = bf16[640,256]{1,0:T(8,128)(2,1)} async-done(((bf16[640,1024]{1,0:T(8,128)(2,1)}), bf16[640,256]{1,0:T(8,128)(2,1)}) %reduce-scatter.27.cloned.1.call-update) | async-done | bytes 327696 | tf_op jit(solution)/shard_map/reduce_scatter | solution.py:32
  860.5 9.7 all-reduce.4
  873.5 7.1 collective-permute-done.6
  882.6 6.5 collective-permute-done.7
  932.7 6.9 reduce-scatter.29.cloned.1.call-done
  941.0 9.7 all-reduce.3
  953.8 7.0 collective-permute-done.9
  962.9 6.5 collective-permute-done.10
  1015.5 28.1 %reduce-scatter.39.cloned.1.call-done = bf16[256,256]{1,0:T(8,128)(2,1)} async-done(((bf16[256,1024]{1,0:T(8,128)(2,1)}), bf16[256,256]{1,0:T(8,128)(2,1)}) %reduce-scatter.39.cloned.1.call-update) | async-done | bytes 131088 | tf_op jit(solution)/shard_map/reduce_scatter | solution.py:286
  1043.5 34.8 %reduce-scatter.35.cloned.1.call-done = bf16[256,3,256]{2,0,1:T(8,128)(2,1)} async-done(((bf16[1024,3,256]{2,0,1:T(8,128)(2,1)}), bf16[256,3,256]{2,0,1:T(8,128)(2,1)}) %reduce-scatter.35.cloned.1.call-update) | async-done | bytes 393232 | tf_op jit(solution)/shard_map/reduce_scatter | solution.py:283
  1078.3 38.4 %reduce-scatter.45.cloned.1.call-done = bf16[1024,256]{1,0:T(8,128)(2,1)} async-done(((bf16[1024,1024]{1,0:T(8,128)(2,1)}), bf16[1024,256]{1,0:T(8,128)(2,1)}) %reduce-scatter.45.cloned.1.call-update) | async-done | bytes 524304 | tf_op jit(solution)/shard_map/reduce_scatter | solution.py:292
  1116.7 38.8 %reduce-scatter.41.cloned.1.call-done = bf16[256,1024]{1,0:T(8,128)(2,1)} async-done(((bf16[1024,1024]{1,0:T(8,128)(2,1)}), bf16[256,1024]{1,0:T(8,128)(2,1)}) %reduce-scatter.41.cloned.1.call-update) | async-done | bytes 524304 | tf_op jit(solution)/shard_map/reduce_scatter | solution.py:289
  1155.5 27.7 %reduce-scatter.37.cloned.1.call-done = bf16[256,256]{1,0:T(8,128)(2,1)} async-done(((bf16[256,1024]{1,0:T(8,128)(2,1)}), bf16[256,256]{1,0:T(8,128)(2,1)}) %reduce-scatter.37.cloned.1.call-update) | async-done | bytes 131088 | tf_op jit(solution)/shard_map/reduce_scatter | solution.py:286
  1183.2 33.9 %reduce-scatter.33.cloned.1.call-done = bf16[256,3,256]{2,0,1:T(8,128)(2,1)} async-done(((bf16[1024,3,256]{2,0,1:T(8,128)(2,1)}), bf16[256,3,256]{2,0,1:T(8,128)(2,1)}) %reduce-scatter.33.cloned.1.call-update) | async-done | bytes 393232 | tf_op jit(solution)/shard_map/reduce_scatter | solution.py:283
  1219.1 31.4 %reduce-scatter.31.cloned.1.call-done = bf16[640,256]{1,0:T(8,128)(2,1)} async-done(((bf16[640,1024]{1,0:T(8,128)(2,1)}), bf16[640,256]{1,0:T(8,128)(2,1)}) %reduce-scatter.31.cloned.1.call-update) | async-done | bytes 327696 | tf_op jit(solution)/shard_map/reduce_scatter | solution.py:32
  1252.0 26.5 %all-reduce.1 = (f32[1,2,256]{2,1,0:T(2,128)S(1)}, f32[1,2,256]{2,1,0:T(2,128)S(1)}, f32[1,2,256]{2,1,0:T(2,128)S(1)}, f32[1,2,256]{2,1,0:T(2,128)S(1)}, f32[1,2...) all-reduce(f32[1,2,256]{2,1,0:T(2,128)S(1)} %maximum_bitcast_fusion, ...), channel_id=1, replica_groups=mesh['dp'=2,'row'=4,'col'=4] {'dp','row'}, use_global_device_ids=true, to_apply=%region_55.57 | all-reduce | flops 6144 | bytes 49152 | tf_op jit(solution)/shard_map/psum | solution.py:302
  1278.5 9.7 all-reduce.2
  (412 shorter events, 261.2 us)
Async XLA Ops:
  7.2 52.3 %all-gather.19.cloned.1.call-start = ((), (), s32[]{:S(2)}) async-start(), calls=%async_computation.16 | async-start | bytes 1638400 | tf_op jit(solution)/shard_map/all_gather | solution.py:46
  8.6 85.9 %copy-start.66 = (f32[1,1,256]{2,1,0:T(1,128)}, f32[1,1,256]{2,1,0:T(1,128)S(1)}, u32[]{:S(2)}) copy-start(f32[1,1,256]{2,1,0:T(1,128)S(1)} %get-tuple-element.118) | copy-start | bytes 3076
  27.7 63.8 %all-gather.27.cloned.1.call-start = ((), (), s32[]{:S(2)}) async-start(), calls=%async_computation.36 | async-start | bytes 1966080 | tf_op jit(solution)/shard_map/all_gather | solution.py:140
  29.8 126.8 %reduce-scatter.17.cloned.1.call-start = ((), (), s32[]{:S(2)}) async-start(), calls=%async_computation.17 | async-start | bytes 3276800 | tf_op jit(solution)/shard_map/reduce_scatter | solution.py:28
  104.4 89.5 %all-gather.29.cloned.1.call-start = ((), (), s32[]{:S(2)}) async-start(), calls=%async_computation.37 | async-start | bytes 2621440 | tf_op jit(solution)/shard_map/all_gather | solution.py:142
  105.5 123.9 %all-gather.21.cloned.1.call-start = ((), (), s32[]{:S(2)}) async-start(), calls=%async_computation.18 | async-start | bytes 1638400 | tf_op jit(solution)/shard_map/all_gather | solution.py:46
  169.3 96.1 %all-gather.31.cloned.1.call-start = ((), (), s32[]{:S(2)}) async-start(), calls=%async_computation.38 | async-start | bytes 2621440 | tf_op jit(solution)/shard_map/all_gather | solution.py:143
  170.4 152.4 %reduce-scatter.19.cloned.1.call-start = ((), (), s32[]{:S(2)}) async-start(), calls=%async_computation.19 | async-start | bytes 3276800 | tf_op jit(solution)/shard_map/reduce_scatter | solution.py:28
  270.5 88.0 %all-gather.33.cloned.1.call-start = ((), (), s32[]{:S(2)}) async-start(), calls=%async_computation.39 | async-start | bytes 1966080 | tf_op jit(solution)/shard_map/all_gather | solution.py:140
  271.2 122.9 %all-gather.23.cloned.1.call-start = ((), (), s32[]{:S(2)}) async-start(), calls=%async_computation.20 | async-start | bytes 1638400 | tf_op jit(solution)/shard_map/all_gather | solution.py:46
  335.5 136.8 %reduce-scatter.21.cloned.1.call-start = ((), (), s32[]{:S(2)}) async-start(), calls=%async_computation.21 | async-start | bytes 3276800 | tf_op jit(solution)/shard_map/reduce_scatter | solution.py:28
  421.6 123.7 %copy-start.81 = (f32[1,1024]{1,0:T(1,128)S(1)}, f32[1,1024]{1,0:T(1,128)}, u32[]{:S(2)}) copy-start(f32[1,1024]{1,0:T(1,128)} %get-tuple-element.112) | copy-start | bytes 12292
  421.6 88.2 %all-gather.35.cloned.1.call-start = ((), (), s32[]{:S(2)}) async-start(), calls=%async_computation.40 | async-start | bytes 2621440 | tf_op jit(solution)/shard_map/all_gather | solution.py:142
  422.3 123.0 %all-gather.25.cloned.1.call-start = ((), (), s32[]{:S(2)}) async-start(), calls=%async_computation.22 | async-start | bytes 1638400 | tf_op jit(solution)/shard_map/all_gather | solution.py:46
  485.0 95.8 %all-gather.37.cloned.1.call-start = ((), (), s32[]{:S(2)}) async-start(), calls=%async_computation.41 | async-start | bytes 2621440 | tf_op jit(solution)/shard_map/all_gather | solution.py:143
  485.8 152.4 %reduce-scatter.23.cloned.1.call-start = ((), (), s32[]{:S(2)}) async-start(), calls=%async_computation.23 | async-start | bytes 3276800 | tf_op jit(solution)/shard_map/reduce_scatter | solution.py:28
  585.9 171.7 %reduce-scatter.25.cloned.1.call-start = ((), (), s32[]{:S(2)}) async-start(), calls=%async_computation.24 | async-start | bytes 1638400 | tf_op jit(solution)/shard_map/reduce_scatter | solution.py:32
  684.1 8.8 collective-permute-start
  693.6 9.5 collective-permute-start.1
  703.2 9.3 collective-permute-start.2
  724.6 134.4 %reduce-scatter.27.cloned.1.call-start = ((), (), s32[]{:S(2)}) async-start(), calls=%async_computation.25 | async-start | bytes 1638400 | tf_op jit(solution)/shard_map/reduce_scatter | solution.py:32
  771.6 8.3 collective-permute-start.3
  779.9 8.7 collective-permute-start.4
  788.6 7.1 collective-permute-start.5
  826.1 113.5 %reduce-scatter.29.cloned.1.call-start = ((), (), s32[]{:S(2)}) async-start(), calls=%async_computation.26 | async-start | bytes 1638400 | tf_op jit(solution)/shard_map/reduce_scatter | solution.py:32
  872.7 7.9 collective-permute-start.6
  880.6 8.5 collective-permute-start.7
  889.1 7.2 collective-permute-start.8
  906.5 108.0 %reduce-scatter.47.cloned.1.call-start = ((), (), s32[]{:S(2)}) async-start(), calls=%async_computation.35 | async-start | bytes 2621440 | tf_op jit(solution)/shard_map/reduce_scatter | solution.py:292
  911.0 104.4 %reduce-scatter.43.cloned.1.call-start = ((), (), s32[]{:S(2)}) async-start(), calls=%async_computation.33 | async-start | bytes 2621440 | tf_op jit(solution)/shard_map/reduce_scatter | solution.py:289
  916.1 127.4 %reduce-scatter.39.cloned.1.call-start = ((), (), s32[]{:S(2)}) async-start(), calls=%async_computation.31 | async-start | bytes 655360 | tf_op jit(solution)/shard_map/reduce_scatter | solution.py:286
  918.5 159.8 %reduce-scatter.35.cloned.1.call-start = ((), (), s32[]{:S(2)}) async-start(), calls=%async_computation.29 | async-start | bytes 1966080 | tf_op jit(solution)/shard_map/reduce_scatter | solution.py:283
  922.8 193.9 %reduce-scatter.45.cloned.1.call-start = ((), (), s32[]{:S(2)}) async-start(), calls=%async_computation.34 | async-start | bytes 2621440 | tf_op jit(solution)/shard_map/reduce_scatter | solution.py:292
  927.5 228.0 %reduce-scatter.41.cloned.1.call-start = ((), (), s32[]{:S(2)}) async-start(), calls=%async_computation.32 | async-start | bytes 2621440 | tf_op jit(solution)/shard_map/reduce_scatter | solution.py:289
  932.6 250.6 %reduce-scatter.37.cloned.1.call-start = ((), (), s32[]{:S(2)}) async-start(), calls=%async_computation.30 | async-start | bytes 655360 | tf_op jit(solution)/shard_map/reduce_scatter | solution.py:286
  953.0 7.8 collective-permute-start.9
  960.8 8.6 collective-permute-start.10
  969.4 7.1 collective-permute-start.11
  985.6 231.5 %reduce-scatter.33.cloned.1.call-start = ((), (), s32[]{:S(2)}) async-start(), calls=%async_computation.28 | async-start | bytes 1966080 | tf_op jit(solution)/shard_map/reduce_scatter | solution.py:283
  1010.5 240.1 %reduce-scatter.31.cloned.1.call-start = ((), (), s32[]{:S(2)}) async-start(), calls=%async_computation.27 | async-start | bytes 1638400 | tf_op jit(solution)/shard_map/reduce_scatter | solution.py:32
  1014.3 204.3 %copy-start.17 = (bf16[640,1,256]{0,2,1:T(8,128)(2,1)S(1)}, bf16[640,1,256]{0,2,1:T(8,128)(2,1)}, u32[]{:S(2)}) copy-start(bf16[640,1,256]{0,2,1:T(8,128)(2,1)} %copy-done.16) | copy-start | bytes 983044
  1014.3 204.4 %copy-start.19 = (bf16[640,1,256]{0,2,1:T(8,128)(2,1)S(1)}, bf16[640,1,256]{0,2,1:T(8,128)(2,1)}, u32[]{:S(2)}) copy-start(bf16[640,1,256]{0,2,1:T(8,128)(2,1)} %copy-done.18) | copy-start | bytes 983044
  1014.3 204.6 %copy-start.20 = (bf16[640,1,256]{0,2,1:T(8,128)(2,1)S(1)}, bf16[640,1,256]{0,2,1:T(8,128)(2,1)}, u32[]{:S(2)}) copy-start(bf16[640,1,256]{0,2,1:T(8,128)(2,1)} %stack_reshape.29) | copy-start | bytes 983044
  1014.3 204.7 %copy-start.21 = (bf16[640,1,256]{0,2,1:T(8,128)(2,1)S(1)}, bf16[640,1,256]{0,2,1:T(8,128)(2,1)}, u32[]{:S(2)}) copy-start(bf16[640,1,256]{0,2,1:T(8,128)(2,1)} %stack_reshape.27) | copy-start | bytes 983044
  1014.3 236.3 %copy-start.46 = (f32[640]{0:T(1024)S(1)}, f32[640]{0:T(1024)}, u32[]{:S(2)}) copy-start(f32[640]{0:T(1024)} %copy-done.45) | copy-start | bytes 7684
  1014.3 236.3 %copy-start.48 = (f32[640]{0:T(1024)S(1)}, f32[640]{0:T(1024)}, u32[]{:S(2)}) copy-start(f32[640]{0:T(1024)} %copy-done.47) | copy-start | bytes 7684
  1014.3 236.3 %copy-start.67 = (f32[1,1,256]{2,1,0:T(1,128)S(1)}, f32[1,1,256]{2,1,0:T(1,128)}, u32[]{:S(2)}) copy-start(f32[1,1,256]{2,1,0:T(1,128)} %copy-done.66) | copy-start | bytes 3076
  1014.3 278.5 %all-reduce.13.cloned.1.call-start = ((), (), s32[]{:S(2)}) async-start(), calls=%async_computation.42 | async-start | bytes 6291456 | tf_op jit(solution)/shard_map/psum | solution.py:297
  (89 other events, 2026.3 us)
Sparse Core Ops, SparseCore 0:
  27.8 31.6 all-gather.18
  61.9 29.4 all-gather.26
  104.5 52.0 reduce-scatter.16
  158.9 34.9 all-gather.28
  195.9 33.4 all-gather.20
  231.6 33.6 all-gather.30
  270.6 52.1 reduce-scatter.18
  325.2 33.2 all-gather.32
  360.6 33.4 all-gather.22
  421.7 50.6 reduce-scatter.20
  474.8 34.9 all-gather.34
  511.8 33.4 all-gather.24
  547.1 33.6 all-gather.36
  586.0 52.0 reduce-scatter.22
  724.7 32.7 reduce-scatter.24
  826.2 32.7 reduce-scatter.26
  906.6 32.9 reduce-scatter.28
  942.4 33.9 reduce-scatter.46
  980.2 35.2 reduce-scatter.42
  1018.7 24.7 reduce-scatter.38
  1047.4 30.9 reduce-scatter.34
  1081.5 35.1 reduce-scatter.44
  1120.3 35.1 reduce-scatter.40
  1158.4 24.7 reduce-scatter.36
  1186.2 30.8 reduce-scatter.32
  1219.3 31.2 reduce-scatter.30
  1253.3 22.3 all-reduce.12
